TPU v7x, 256 devices: a whole 4x4x8 slice. The times are simulated.
256 devices in a mesh: dp: 16 (over x, y_hi, core), expert: 16 (over y_lo, z).
Axes of the slice: x: 4, y: 4 (y_hi: 2, y_lo: 2; y = y_hi * 2 + y_lo), z: 8, core: 2. Of those that a mesh axis runs over, the one named last changes fastest.
Arguments:
- tokens: bfloat16 [32768, 1024], P(('dp', 'expert')), may hold values from -6 to 6
- expert_ids: int32 [32768, 8], P(('dp', 'expert')), may hold values from 0 to 63, all different within a row; in each aligned block of 128 rows (0 to 127, 128 to 255, ...) at most 24 rows name the same one
- upstream: bfloat16 [32768, 1024], P(('dp', 'expert')), may hold values from -6 to 6
- router_weight: bfloat16 [1024, 64], replicated, may hold values from -0.1875 to 0.1875
- gate_matrix: bfloat16 [64, 384, 1024], P('expert'), may hold values from -0.1875 to 0.1875
- up_matrix: bfloat16 [64, 384, 1024], P('expert'), may hold values from -0.1875 to 0.1875
- down_matrix: bfloat16 [64, 384, 1024], P('expert'), may hold values from -0.3125 to 0.3125
Outputs:
- mixture: bfloat16 [32768, 1024], P(('dp', 'expert'))
- input_grad: bfloat16 [32768, 1024], P(('dp', 'expert'))
- router_grad: float32 [1024, 64], replicated
- gate_grad: float32 [64, 384, 1024], P('expert', 'dp')
- up_grad: float32 [64, 384, 1024], P('expert', 'dp')
- down_grad: float32 [64, 384, 1024], P('expert', 'dp')
Inputs may be any that keep to these rules, and one draw needn't show every extreme that they name: `expert_ids`: each row names 8 different experts. Among the rows of one device no expert is named more than 24 times, a bound that some block reaches.
All inputs are finite; a program needn't handle non-finite values.
Results may differ from a plain program's by a relative error of at most 0.0063.
Values may be sent and summed in bfloat16 or wider, within the bound.
No kernel may reach another device: no remote copies, remote signals or barrier semaphores. Data moves between devices by JAX's collectives and lax.ppermute only.
A program may use at most 320 MiB of HBM per device.

v0:
```python
import jax
import jax.numpy as jnp
from jax import lax
from jax.sharding import PartitionSpec as P


def slot_positions(expert_ids, experts, capacity):
    flat_ids = expert_ids.reshape(-1)
    columns = lax.broadcasted_iota(jnp.int32, (1, experts), 1)
    onehot = (flat_ids[:, None] == columns).astype(jnp.int32)
    ranking = jnp.cumsum(onehot, axis=0) - 1
    slot_numbers = jnp.sum(ranking * onehot, axis=1)
    return flat_ids * capacity + slot_numbers


def slot_sources(positions, total_slots):
    assign_count = positions.shape[0]
    return (
        jnp.full((total_slots,), -1, jnp.int32)
        .at[positions]
        .set(jnp.arange(assign_count, dtype=jnp.int32))
    )


def fill_slots(source_rows, sources, divisor):
    occupied = sources >= 0
    picked = jnp.take(source_rows, jnp.maximum(sources, 0) // divisor, axis=0)
    return jnp.where(occupied[:, None], picked, jnp.zeros_like(picked))


def backward_local(pre_gate, pre_up, logistic, act_grad):
    gate_back = (act_grad * pre_up * logistic * (1.0 + pre_gate * (1.0 - logistic))).astype(
        jnp.bfloat16
    )
    up_back = (act_grad * (pre_gate * logistic)).astype(jnp.bfloat16)
    return (gate_back, up_back)


def body(tokens, expert_ids, upstream, router_weight, gate_matrix, up_matrix, down_matrix):
    tok_rows, model_width = tokens.shape
    per_token = expert_ids.shape[1]
    exp_dev, hidden = (gate_matrix.shape[0], gate_matrix.shape[1])
    expert_peers = lax.axis_size("expert")
    experts = expert_peers * exp_dev
    capacity = tok_rows * per_token * 3 // (2 * experts)
    positions = slot_positions(expert_ids, experts, capacity)
    sources = slot_sources(positions, experts * capacity)
    send_rows = fill_slots(tokens, sources, per_token).reshape(
        expert_peers, exp_dev * capacity, model_width
    )
    recv_rows = lax.all_to_all(send_rows, "expert", split_axis=0, concat_axis=0, tiled=True)
    expert_rows = recv_rows.reshape(expert_peers, exp_dev, capacity, model_width)
    pre_gate = jnp.einsum(
        "secd,efd->secf", expert_rows, gate_matrix, preferred_element_type=jnp.float32
    )
    pre_up = jnp.einsum(
        "secd,efd->secf", expert_rows, up_matrix, preferred_element_type=jnp.float32
    )
    logistic = jax.nn.sigmoid(pre_gate)
    activated = (pre_gate * logistic * pre_up).astype(jnp.bfloat16)
    produced = jnp.einsum(
        "secf,efd->secd", activated, down_matrix, preferred_element_type=jnp.float32
    ).astype(jnp.bfloat16)
    returned = lax.all_to_all(
        produced.reshape(expert_peers, exp_dev * capacity, model_width),
        "expert",
        split_axis=0,
        concat_axis=0,
        tiled=True,
    )
    assign_out = jnp.take(returned.reshape(experts * capacity, model_width), positions, axis=0)
    assign_out = assign_out.reshape(tok_rows, per_token, model_width).astype(jnp.float32)
    logits = jnp.dot(tokens, router_weight, preferred_element_type=jnp.float32)
    chosen = jnp.take_along_axis(logits, expert_ids, axis=1)
    raised = jnp.exp(chosen)
    gate_probs = raised / jnp.sum(raised, axis=1, keepdims=True)
    mixture = jnp.sum(gate_probs[:, :, None] * assign_out, axis=1).astype(jnp.bfloat16)
    cotangent = upstream.astype(jnp.float32)
    prob_grad = jnp.sum(cotangent[:, None, :] * assign_out, axis=2)
    centered = prob_grad - jnp.sum(gate_probs * prob_grad, axis=1, keepdims=True)
    chosen_grad = gate_probs * centered
    expert_cols = lax.broadcasted_iota(jnp.int32, (1, 1, experts), 2)
    logit_grad = jnp.sum(
        jnp.where(expert_ids[:, :, None] == expert_cols, chosen_grad[:, :, None], 0.0), axis=1
    )
    router_part = jnp.dot(tokens.astype(jnp.float32).T, logit_grad, precision=lax.Precision.HIGHEST)
    router_grad = lax.psum(router_part, ("dp", "expert"))
    router_input = jnp.dot(
        logit_grad, router_weight.astype(jnp.float32).T, precision=lax.Precision.HIGHEST
    )
    out_grad = (gate_probs[:, :, None] * cotangent[:, None, :]).astype(jnp.bfloat16)
    out_grad = out_grad.reshape(tok_rows * per_token, model_width)
    send_grad = fill_slots(out_grad, sources, 1).reshape(
        expert_peers, exp_dev * capacity, model_width
    )
    recv_grad = lax.all_to_all(send_grad, "expert", split_axis=0, concat_axis=0, tiled=True)
    grad_rows = recv_grad.reshape(expert_peers, exp_dev, capacity, model_width)
    act_grad = jnp.einsum(
        "secd,efd->secf", grad_rows, down_matrix, preferred_element_type=jnp.float32
    )
    gate_back, up_back = backward_local(pre_gate, pre_up, logistic, act_grad)
    row_grad = (
        jnp.einsum("secf,efd->secd", gate_back, gate_matrix, preferred_element_type=jnp.float32)
        + jnp.einsum("secf,efd->secd", up_back, up_matrix, preferred_element_type=jnp.float32)
    ).astype(jnp.bfloat16)
    returned_grads = lax.all_to_all(
        row_grad.reshape(expert_peers, exp_dev * capacity, model_width),
        "expert",
        split_axis=0,
        concat_axis=0,
        tiled=True,
    )
    per_assign = jnp.take(
        returned_grads.reshape(experts * capacity, model_width), positions, axis=0
    )
    per_assign = per_assign.reshape(tok_rows, per_token, model_width).astype(jnp.float32)
    input_grad = (jnp.sum(per_assign, axis=1) + router_input).astype(jnp.bfloat16)
    full_gate = jnp.einsum(
        "secf,secd->efd", gate_back, expert_rows, preferred_element_type=jnp.float32
    )
    full_up = jnp.einsum("secf,secd->efd", up_back, expert_rows, preferred_element_type=jnp.float32)
    full_down = jnp.einsum(
        "secf,secd->efd", activated, grad_rows, preferred_element_type=jnp.float32
    )
    gate_grad = lax.psum_scatter(full_gate, "dp", scatter_dimension=1, tiled=True)
    up_grad = lax.psum_scatter(full_up, "dp", scatter_dimension=1, tiled=True)
    down_grad = lax.psum_scatter(full_down, "dp", scatter_dimension=1, tiled=True)
    return (mixture, input_grad, router_grad, gate_grad, up_grad, down_grad)


def solution(mesh):
    in_specs = (
        P(("dp", "expert"), None),
        P(("dp", "expert"), None),
        P(("dp", "expert"), None),
        P(),
        P("expert", None, None),
        P("expert", None, None),
        P("expert", None, None),
    )
    out_specs = (
        P(("dp", "expert"), None),
        P(("dp", "expert"), None),
        P(),
        P("expert", "dp", None),
        P("expert", "dp", None),
        P("expert", "dp", None),
    )
    return jax.shard_map(body, mesh=mesh, in_specs=in_specs, out_specs=out_specs, check_vma=False)
```

profile of v0, /device:TPU:2, one launch (start us, length us, event | category | flops | bytes accessed | tf_op | source)
XLA Modules:
  0.0 670.4 jit_solution(13618022292784977458)
XLA Ops:
  10.9 34.2 %reduce-window.6 = s32[64,8,128]{2,1,0:T(8,128)} reduce-window(s32[64,8,128]{2,1,0:T(8,128)} %fusion.43, s32[]{:T(128)} %constant.85.clone.1), window={size=1x1x128 pad=0_0x0_0x127_0}, to_apply=%region_1.2 | reduce-window | flops 8323072 | bytes 524292 | tf_op jit(solution)/shard_map/reduce-window
  49.3 4.3 scatter_custom_fusion
  53.8 5.8 gather_fusion
  61.9 81.5 %all_to_all.20 = bf16[16,96,1024]{2,1,0:T(8,128)(2,1)S(1)} all-to-all(bf16[16,96,1024]{2,1,0:T(8,128)(2,1)S(1)} %select_select_fusion.1), channel_id=1, replica_groups=mesh['dp'=16,'expert'=16] {'expert'}, dimensions={0} | all-to-all | bytes 6291456 | tf_op jit(solution)/shard_map/all_to_all | solution.py:51
  146.4 3.5 fusion.27
  153.9 4.8 all-to-all-start.1
  160.0 7.0 %gather_fusion.2 = f32[1024]{0:T(1024)S(1)} fusion(f32[128,64]{0,1:T(8,128)S(1)} %fusion.48, s32[1024]{0:T(1024)S(1)} %reshape.214), kind=kCustom, calls=%fused_computation.4 | custom fusion | bytes 16384 | tf_op jit(solution)/shard_map/jit(take_along_axis)/gather | solution.py:74
  169.2 61.6 %all-to-all-done.1 = bf16[16,96,1024]{2,1,0:T(8,128)(2,1)} async-done(((bf16[16,96,1024]{2,1,0:T(8,128)(2,1)}), bf16[16,96,1024]{2,1,0:T(8,128)(2,1)}, u32[]{:S(2)}, u32[]{:S(2)}) %all-to-all-start.1) | async-done | bytes 3145760 | tf_op jit(solution)/shard_map/all_to_all | solution.py:64
  230.8 8.3 %gather_fusion.3 = bf16[1024,1024]{1,0:T(8,128)(2,1)} fusion(bf16[1536,1024]{1,0:T(8,128)(2,1)} %bitcast.17, s32[1024]{0:T(1024)S(1)} %broadcast_clamp_fusion), kind=kCustom, calls=%fused_computation.clone | custom fusion | bytes 4198400 | tf_op jit(solution)/shard_map/jit(_take)/gather | solution.py:71
  242.1 2.7 fusion.2
  244.8 9.6 %gather_fusion.1 = bf16[1536,1024]{1,0:T(8,128)(2,1)} fusion(bf16[1024,1024]{1,0:T(8,128)(2,1)} %fusion.2, s32[2048]{0:T(1024)S(1)} %pad_clamp_fusion), kind=kCustom, calls=%fused_computation.3 | custom fusion | bytes 6297600 | tf_op jit(solution)/shard_map/jit(_take)/gather | solution.py:27
  254.4 3.4 select_select_fusion
  257.8 7.5 %all-to-all-start.2 = ((bf16[16,96,1024]{2,1,0:T(8,128)(2,1)}), bf16[16,96,1024]{2,1,0:T(8,128)(2,1)}, u32[]{:S(2)}, u32[]{:S(2)}) async-start(bf16[16,96,1024]{2,1,0:T(8,128)(2,1)} %select_select_fusion), calls=%async_computation.2 | async-start | bytes 6291456 | tf_op jit(solution)/shard_map/all_to_all | solution.py:96
  266.4 69.4 %all-to-all-done.2 = bf16[16,96,1024]{2,1,0:T(8,128)(2,1)} async-done(((bf16[16,96,1024]{2,1,0:T(8,128)(2,1)}), bf16[16,96,1024]{2,1,0:T(8,128)(2,1)}, u32[]{:S(2)}, u32[]{:S(2)}) %all-to-all-start.2) | async-done | bytes 3145760 | tf_op jit(solution)/shard_map/all_to_all | solution.py:96
  335.8 6.8 %fusion.20 = f32[4,384,1024]{2,1,0:T(8,128)} fusion(bf16[16,4,24,384]{3,2,0,1:T(8,128)(2,1)} %copy-done.7, bf16[16,4,24,1024]{3,2,1,0:T(8,128)(2,1)} %bitcast.21), kind=kOutput, calls=%fused_computation.34 | convolution fusion | flops 1207959552 | bytes 10616832 | tf_op jit(solution)/shard_map/secf,secd->efd/dot_general | solution.py:122
  342.7 6.8 %fusion.25 = (bf16[16,4,24,384]{3,2,0,1:T(8,128)(2,1)S(1)}, bf16[16,4,24,384]{3,2,0,1:T(8,128)(2,1)}) fusion(f32[4,16,24,384]{3,2,1,0:T(8,128)} %get-tuple-element.18, f32[4,16,24,384]{3,2,1,0:T(8,128)} %copy-done.12, bf16[4,384,1024]{2,1,0:T(8,128)(2,1)S(1)} %copy-done, bf16[16,4,24,1024]{3,2,1,0:T(8,128)(2,1)} %bitcast.21), kind=kOutput, calls=%fused_computation.41 | convolution fusion | flops 1215627264 | bytes 13369344 | tf_op jit(solution)/shard_map/secd,efd->secf/dot_general | solution.py:98
  350.6 4.5 convolution_bitcast_fusion.1
  355.4 6.8 %convolution_bitcast_fusion = f32[4,384,1024]{2,1,0:T(8,128)} fusion(bf16[16,4,24,384]{3,2,0,1:T(8,128)(2,1)} %get-tuple-element.14, bf16[16,4,24,1024]{3,2,1,0:T(8,128)(2,1)} %bitcast.146), kind=kOutput, calls=%fused_computation.35 | convolution fusion | flops 1207959552 | bytes 10616832 | tf_op jit(solution)/shard_map/secf,secd->efd/dot_general | solution.py:121
  362.2 4.5 fusion.5
  368.9 81.1 %all_to_all.21 = bf16[16,96,1024]{2,1,0:T(8,128)(2,1)} all-to-all(bf16[16,96,1024]{2,1,0:T(8,128)(2,1)S(1)} %bitcast.141), channel_id=1, replica_groups=mesh['dp'=16,'expert'=16] {'expert'}, dimensions={0} | all-to-all | bytes 6291456 | tf_op jit(solution)/shard_map/all_to_all | solution.py:106
  450.0 8.4 %gather_fusion.4 = bf16[1024,1024]{1,0:T(8,128)(2,1)} fusion(bf16[1536,1024]{1,0:T(8,128)(2,1)} %bitcast.139, s32[1024]{0:T(1024)S(1)} %broadcast_clamp_fusion), kind=kCustom, calls=%fused_computation.1.clone | custom fusion | bytes 4198400 | tf_op jit(solution)/shard_map/jit(_take)/gather | solution.py:113
  458.3 5.2 convert_reduce_fusion
  464.7 101.7 %all-reduce.2.cloned.1.call-done = f32[1024,64]{0,1:T(8,128)} async-done(((f32[1024,64]{0,1:T(8,128)}), f32[1024,64]{0,1:T(8,128)}) %all-reduce.2.cloned.1.call-update) | async-done | bytes 262160 | tf_op jit(solution)/shard_map/psum | solution.py:87
  566.4 94.6 %reduce-scatter.6.cloned.1.call-done = f32[4,24,1024]{2,1,0:T(8,128)} async-done(((f32[4,384,1024]{2,1,0:T(8,128)}), f32[4,24,1024]{2,1,0:T(8,128)}) %reduce-scatter.6.cloned.1.call-update) | async-done | bytes 393232 | tf_op jit(solution)/shard_map/reduce_scatter | solution.py:126
  (86 shorter events, 30.3 us)
Async XLA Ops:
  8.0 141.9 %copy-start = (bf16[4,384,1024]{2,1,0:T(8,128)(2,1)S(1)}, bf16[4,384,1024]{2,1,0:T(8,128)(2,1)}, u32[]{:S(2)}) copy-start(bf16[4,384,1024]{2,1,0:T(8,128)(2,1)} %param.15) | copy-start | bytes 9437188
  8.0 45.8 %copy-start.1 = (bf16[128,1024]{1,0:T(8,128)(2,1)S(1)}, bf16[128,1024]{1,0:T(8,128)(2,1)}, u32[]{:S(2)}) copy-start(bf16[128,1024]{1,0:T(8,128)(2,1)} %param.9) | copy-start | bytes 786436
  61.8 81.5 %copy-start.4 = (bf16[4,384,1024]{2,1,0:T(8,128)(2,1)S(1)}, bf16[4,384,1024]{2,1,0:T(8,128)(2,1)}, u32[]{:S(2)}) copy-start(bf16[4,384,1024]{2,1,0:T(8,128)(2,1)} %param.13) | copy-start | bytes 9437188
  143.4 1.9 copy-start.2
  143.4 3.0 copy-start.6
  146.4 3.5 copy-start.12
  149.9 1.8 copy-start.7
  153.9 4.8 copy-start.11
  153.9 76.9 %all-to-all-start.1 = ((bf16[16,96,1024]{2,1,0:T(8,128)(2,1)}), bf16[16,96,1024]{2,1,0:T(8,128)(2,1)}, u32[]{:S(2)}, u32[]{:S(2)}) async-start(bf16[16,96,1024]{2,1,0:T(8,128)(2,1)} %bitcast.140), calls=%async_computation.1 | async-start | bytes 6291456 | tf_op jit(solution)/shard_map/all_to_all | solution.py:64
  257.8 78.0 %all-to-all-start.2 = ((bf16[16,96,1024]{2,1,0:T(8,128)(2,1)}), bf16[16,96,1024]{2,1,0:T(8,128)(2,1)}, u32[]{:S(2)}, u32[]{:S(2)}) async-start(bf16[16,96,1024]{2,1,0:T(8,128)(2,1)} %select_select_fusion), calls=%async_computation.2 | async-start | bytes 6291456 | tf_op jit(solution)/shard_map/all_to_all | solution.py:96
  265.2 301.2 %all-reduce.2.cloned.1.call-start = ((), (), s32[]{:S(2)}) async-start(), calls=%async_computation.7 | async-start | bytes 524288 | tf_op jit(solution)/shard_map/psum | solution.py:87
  266.3 300.1 %reduce-scatter.8.cloned.1.call-start = ((), (), s32[]{:S(2)}) async-start(), calls=%async_computation.10 | async-start | bytes 6684672 | tf_op jit(solution)/shard_map/reduce_scatter | solution.py:127
  342.6 223.9 %reduce-scatter.4.cloned.1.call-start = ((), (), s32[]{:S(2)}) async-start(), calls=%async_computation.8 | async-start | bytes 6684672 | tf_op jit(solution)/shard_map/reduce_scatter | solution.py:125
  342.6 7.9 %copy-start.3 = (bf16[16,96,1024]{2,1,0:T(8,128)(2,1)S(1)}, bf16[16,96,1024]{2,1,0:T(8,128)(2,1)}, u32[]{:S(2)}) copy-start(bf16[16,96,1024]{2,1,0:T(8,128)(2,1)} %copy-done.2) | copy-start | bytes 9437188
  349.5 1.1 copy-start.8
  355.1 306.0 %reduce-scatter.6.cloned.1.call-start = ((), (), s32[]{:S(2)}) async-start(), calls=%async_computation.9 | async-start | bytes 6684672 | tf_op jit(solution)/shard_map/reduce_scatter | solution.py:126
  362.2 4.6 copy-start.5
  362.2 4.6 copy-start.9
  458.3 5.2 copy-start.10
Sparse Core Ops, SparseCore 0:
  272.1 294.2 all-reduce.1
Sparse Core Ops, SparseCore 1:
  342.7 116.4 reduce-scatter.7
  464.0 96.0 reduce-scatter.3
  565.0 96.1 reduce-scatter.5
where the time goes:
time: 673 us; the launch traced here: 670 us
  waiting for transfers between devices  327 us (49%)
  blocking collectives  163 us (24%)
  local copies, waits for them, and re-layouts  55.1 us (8%)
  other arithmetic  54.9 us (8%)
  matrix products  41.6 us (6%)
  between operations  16 us (2%)
  starting transfers between devices  12.7 us (2%)
    psum x1, waiting for transfers between devices, body(): router_grad = lax.psum(router_part, ('dp', 'expert'))  102 us
    reduce_scatter x1, waiting for transfers between devices, body(): up_grad = lax.psum_scatter(full_up, 'dp', scatter_dimension=1, tiled=True)  94.6 us
    all_to_all x1, blocking collectives, body(): lax.all_to_all(send_rows, 'expert', split_axis=0, concat_axis=0, tiled=True)  81.5 us
    all_to_all x1, blocking collectives, body(): lax.all_to_all(row_grad.reshape(expert_peers, exp_dev * capacity, model_w...  81.1 us
    all_to_all x1, waiting for transfers between devices, body(): lax.all_to_all(send_grad, 'expert', split_axis=0, concat_axis=0, tiled=True)  69.4 us
    all_to_all x1, waiting for transfers between devices, body(): lax.all_to_all(produced.reshape(expert_peers, exp_dev * capacity, model_w...  61.6 us
    another operation x2, other arithmetic  34.2 us
    gather x2, local copies, waits for them, and re-layouts, fill_slots(): picked = jnp.take(source_rows, jnp.maximum(sources, 0) // divisor, axis=0)  15.5 us
  transfers between devices with their start and end apart: 6, of which 4 were waited for; matrix products, arithmetic and copies ran while one was open for 9% of the time, Pallas kernels for 0%

commit v1 on v0

--- a/solution.py
+++ b/solution.py
@@ -84,7 +84,7 @@
         jnp.where(expert_ids[:, :, None] == expert_cols, chosen_grad[:, :, None], 0.0), axis=1
     )
     router_part = jnp.dot(tokens.astype(jnp.float32).T, logit_grad, precision=lax.Precision.HIGHEST)
-    router_grad = lax.psum(router_part, ("dp", "expert"))
+    router_grad = lax.psum(lax.psum(router_part, "dp"), "expert")
     router_input = jnp.dot(
         logit_grad, router_weight.astype(jnp.float32).T, precision=lax.Precision.HIGHEST
     )

time: 673 us -> 877 us (1.30)
  waiting for transfers between devices: 327 us -> 535 us
    reduce_scatter x1, waiting for transfers between devices: 0.01 us -> 101 us  [body(): lax.psum_scatter(full_gate, 'dp', scatter_dimension=1, tiled=True)]
    reduce_scatter x1, waiting for transfers between devices: 0.01 us -> 100 us  [body(): lax.psum_scatter(full_down, 'dp', scatter_dimension=1, tiled=True)]
    all_to_all x1, waiting for transfers between devices: 69.4 us -> 0.01 us  [body(): lax.all_to_all(send_grad, 'expert', split_axis=0, concat_axis=0, tiled=True)]
    psum x1 -> x2, waiting for transfers between devices: 102 us -> 171 us  [body(): router_grad = lax.psum(lax.psum(router_part, 'dp'), 'expert')]
  transfers between devices with their start and end apart: 6 -> 7, of which waited for: 4 -> 6; matrix products, arithmetic and copies ran while one was open for 9% -> 7% of each run, Pallas kernels for 0% -> 0%
where the time goes in v1:
time: 877 us; the launch traced here: 875 us
  waiting for transfers between devices  535 us (61%)
  blocking collectives  162 us (18%)
  local copies, waits for them, and re-layouts  55.1 us (6%)
  other arithmetic  54.9 us (6%)
  matrix products  41.1 us (5%)
  between operations  14.1 us (2%)
  starting transfers between devices  12.7 us (1%)
    psum x2, waiting for transfers between devices, body(): router_grad = lax.psum(lax.psum(router_part, 'dp'), 'expert')  171 us
    reduce_scatter x1, waiting for transfers between devices, body(): up_grad = lax.psum_scatter(full_up, 'dp', scatter_dimension=1, tiled=True)  101 us
    reduce_scatter x1, waiting for transfers between devices, body(): lax.psum_scatter(full_gate, 'dp', scatter_dimension=1, tiled=True)  101 us
    reduce_scatter x1, waiting for transfers between devices, body(): lax.psum_scatter(full_down, 'dp', scatter_dimension=1, tiled=True)  100 us
    all_to_all x1, blocking collectives, body(): lax.all_to_all(send_rows, 'expert', split_axis=0, concat_axis=0, tiled=True)  81.5 us
    all_to_all x1, blocking collectives, body(): lax.all_to_all(row_grad.reshape(expert_peers, exp_dev * capacity, model_w...  80.5 us
    all_to_all x1, waiting for transfers between devices, body(): lax.all_to_all(produced.reshape(expert_peers, exp_dev * capacity, model_w...  61.6 us
    another operation x2, other arithmetic  34.2 us
  transfers between devices with their start and end apart: 7, of which 6 were waited for; matrix products, arithmetic and copies ran while one was open for 7% of the time, Pallas kernels for 0%

profile of v1, /device:TPU:2, one launch (start us, length us, event | category | flops | bytes accessed | tf_op | source)
XLA Modules:
  0.0 874.7 jit_solution(7259287915859522930)
XLA Ops:
  10.1 34.2 %reduce-window.6 = s32[64,8,128]{2,1,0:T(8,128)} reduce-window(s32[64,8,128]{2,1,0:T(8,128)} %fusion.43, s32[]{:T(128)} %constant.85.clone.1), window={size=1x1x128 pad=0_0x0_0x127_0}, to_apply=%region_1.2 | reduce-window | flops 8323072 | bytes 524292 | tf_op jit(solution)/shard_map/reduce-window
  48.4 4.3 scatter_custom_fusion
  53.0 5.8 gather_fusion
  61.0 81.5 %all_to_all.20 = bf16[16,96,1024]{2,1,0:T(8,128)(2,1)S(1)} all-to-all(bf16[16,96,1024]{2,1,0:T(8,128)(2,1)S(1)} %select_select_fusion.1), channel_id=1, replica_groups=mesh['dp'=16,'expert'=16] {'expert'}, dimensions={0} | all-to-all | bytes 6291456 | tf_op jit(solution)/shard_map/all_to_all | solution.py:51
  145.6 3.5 fusion.27
  153.1 4.8 all-to-all-start.1
  159.2 7.0 gather_fusion.2
  168.4 61.6 %all-to-all-done.1 = bf16[16,96,1024]{2,1,0:T(8,128)(2,1)} async-done(((bf16[16,96,1024]{2,1,0:T(8,128)(2,1)}), bf16[16,96,1024]{2,1,0:T(8,128)(2,1)}, u32[]{:S(2)}, u32[]{:S(2)}) %all-to-all-start.1) | async-done | bytes 3145760 | tf_op jit(solution)/shard_map/all_to_all | solution.py:64
  230.0 8.3 gather_fusion.3
  243.9 9.6 %gather_fusion.1 = bf16[1536,1024]{1,0:T(8,128)(2,1)} fusion(bf16[1024,1024]{1,0:T(8,128)(2,1)} %fusion.2, s32[2048]{0:T(1024)S(1)} %pad_clamp_fusion), kind=kCustom, calls=%fused_computation.3 | custom fusion | bytes 6297600 | tf_op jit(solution)/shard_map/jit(_take)/gather | solution.py:27
  256.9 7.5 all-to-all-start.2
  265.6 143.3 %all-reduce.3.cloned.1.call-done = f32[1024,64]{0,1:T(8,128)} async-done(((f32[1024,64]{0,1:T(8,128)}), f32[1024,64]{0,1:T(8,128)}) %all-reduce.3.cloned.1.call-update) | async-done | bytes 262160 | tf_op jit(solution)/shard_map/psum | solution.py:87
  408.9 6.7 fusion.20
  415.7 6.8 fusion.25
  423.6 4.5 convolution_bitcast_fusion.1
  428.4 6.7 convolution_bitcast_fusion
  435.2 4.2 fusion.5
  441.5 80.5 %all_to_all.21 = bf16[16,96,1024]{2,1,0:T(8,128)(2,1)} all-to-all(bf16[16,96,1024]{2,1,0:T(8,128)(2,1)S(1)} %bitcast.141), channel_id=1, replica_groups=mesh['dp'=16,'expert'=16] {'expert'}, dimensions={0} | all-to-all | bytes 6291456 | tf_op jit(solution)/shard_map/all_to_all | solution.py:106
  522.1 8.3 gather_fusion.4
  530.4 5.2 convert_reduce_fusion
  536.8 27.5 %all-reduce.5.cloned.1.call-done = f32[1024,64]{0,1:T(8,128)} async-done(((f32[1024,64]{0,1:T(8,128)}), f32[1024,64]{0,1:T(8,128)}) %all-reduce.5.cloned.1.call-update) | async-done | bytes 262160 | tf_op jit(solution)/shard_map/psum | solution.py:87
  564.3 100.1 %reduce-scatter.8.cloned.1.call-done = f32[4,24,1024]{2,1,0:T(8,128)} async-done(((f32[4,384,1024]{2,1,0:T(8,128)}), f32[4,24,1024]{2,1,0:T(8,128)}) %reduce-scatter.8.cloned.1.call-update) | async-done | bytes 393232 | tf_op jit(solution)/shard_map/reduce_scatter | solution.py:127
  664.4 101.0 %reduce-scatter.4.cloned.1.call-done = f32[4,24,1024]{2,1,0:T(8,128)} async-done(((f32[4,384,1024]{2,1,0:T(8,128)}), f32[4,24,1024]{2,1,0:T(8,128)}) %reduce-scatter.4.cloned.1.call-update) | async-done | bytes 393232 | tf_op jit(solution)/shard_map/reduce_scatter | solution.py:125
  765.4 101.1 %reduce-scatter.6.cloned.1.call-done = f32[4,24,1024]{2,1,0:T(8,128)} async-done(((f32[4,384,1024]{2,1,0:T(8,128)}), f32[4,24,1024]{2,1,0:T(8,128)}) %reduce-scatter.6.cloned.1.call-update) | async-done | bytes 393232 | tf_op jit(solution)/shard_map/reduce_scatter | solution.py:126
  (89 shorter events, 36.4 us)
Async XLA Ops:
  7.2 141.9 %copy-start = (bf16[4,384,1024]{2,1,0:T(8,128)(2,1)S(1)}, bf16[4,384,1024]{2,1,0:T(8,128)(2,1)}, u32[]{:S(2)}) copy-start(bf16[4,384,1024]{2,1,0:T(8,128)(2,1)} %param.15) | copy-start | bytes 9437188
  7.2 45.8 %copy-start.1 = (bf16[128,1024]{1,0:T(8,128)(2,1)S(1)}, bf16[128,1024]{1,0:T(8,128)(2,1)}, u32[]{:S(2)}) copy-start(bf16[128,1024]{1,0:T(8,128)(2,1)} %param.9) | copy-start | bytes 786436
  61.0 81.5 %copy-start.4 = (bf16[4,384,1024]{2,1,0:T(8,128)(2,1)S(1)}, bf16[4,384,1024]{2,1,0:T(8,128)(2,1)}, u32[]{:S(2)}) copy-start(bf16[4,384,1024]{2,1,0:T(8,128)(2,1)} %param.13) | copy-start | bytes 9437188
  142.5 1.9 copy-start.2
  142.6 3.0 copy-start.6
  145.6 3.5 copy-start.12
  149.1 1.8 copy-start.7
  153.0 4.8 copy-start.11
  153.1 76.9 %all-to-all-start.1 = ((bf16[16,96,1024]{2,1,0:T(8,128)(2,1)}), bf16[16,96,1024]{2,1,0:T(8,128)(2,1)}, u32[]{:S(2)}, u32[]{:S(2)}) async-start(bf16[16,96,1024]{2,1,0:T(8,128)(2,1)} %bitcast.140), calls=%async_computation.1 | async-start | bytes 6291456 | tf_op jit(solution)/shard_map/all_to_all | solution.py:64
  256.9 152.0 %all-to-all-start.2 = ((bf16[16,96,1024]{2,1,0:T(8,128)(2,1)}), bf16[16,96,1024]{2,1,0:T(8,128)(2,1)}, u32[]{:S(2)}, u32[]{:S(2)}) async-start(bf16[16,96,1024]{2,1,0:T(8,128)(2,1)} %select_select_fusion), calls=%async_computation.2 | async-start | bytes 6291456 | tf_op jit(solution)/shard_map/all_to_all | solution.py:96
  264.4 144.4 %all-reduce.3.cloned.1.call-start = ((), (), s32[]{:S(2)}) async-start(), calls=%async_computation.7 | async-start | bytes 524288 | tf_op jit(solution)/shard_map/psum | solution.py:87
  265.5 298.7 %all-reduce.5.cloned.1.call-start = ((), (), s32[]{:S(2)}) async-start(), calls=%async_computation.8 | async-start | bytes 524288 | tf_op jit(solution)/shard_map/psum | solution.py:87
  408.9 255.5 %reduce-scatter.8.cloned.1.call-start = ((), (), s32[]{:S(2)}) async-start(), calls=%async_computation.11 | async-start | bytes 6684672 | tf_op jit(solution)/shard_map/reduce_scatter | solution.py:127
  415.7 349.7 %reduce-scatter.4.cloned.1.call-start = ((), (), s32[]{:S(2)}) async-start(), calls=%async_computation.9 | async-start | bytes 6684672 | tf_op jit(solution)/shard_map/reduce_scatter | solution.py:125
  415.7 7.9 copy-start.3
  422.5 1.1 copy-start.8
  428.1 438.3 %reduce-scatter.6.cloned.1.call-start = ((), (), s32[]{:S(2)}) async-start(), calls=%async_computation.10 | async-start | bytes 6684672 | tf_op jit(solution)/shard_map/reduce_scatter | solution.py:126
  435.1 4.2 copy-start.5
  435.2 4.2 copy-start.9
  530.4 5.2 copy-start.10
Sparse Core Ops, SparseCore 0:
  268.4 140.3 all-reduce.2
  411.6 152.5 all-reduce.4
  569.3 95.0 reduce-scatter.7
  669.3 96.1 reduce-scatter.3
  770.3 96.1 reduce-scatter.5
